TPU v7x, 128 devices: a whole 4x4x4 slice. The times are simulated.
128 devices in a mesh: rows: 32 (over z, y, core), vecs: 4 (over x).
Axes of the slice: x: 4, y: 4, z: 4, core: 2. Of those that a mesh axis runs over, the one named last changes fastest.
Arguments:
- vectors: bfloat16 [131072, 1024], P('rows', 'vecs'), may hold values from -6 to 6, as said below
- blocks: bfloat16 [1024, 5, 128, 128], P('rows'), may hold values from -0.25 to 0.25
- columns: int32 [1024, 5], P('rows'), may hold values from 0 to 1023, as said below
Outputs:
- basis: float32 [131072, 1024], P('rows', 'vecs')
Inputs may be any that keep to these rules, and one draw needn't show every extreme that they name: Each block row i names 5 block columns of the form i + d clipped to 0 .. 1023, with distinct d in -8 .. 8; near the grid's ends some may repeat. `vectors`: entries of order one.
All inputs are finite; a program needn't handle non-finite values.
Results may differ from a plain program's by a relative error of at most 0.0075.
Values may be sent and summed in bfloat16 or wider, within the bound.
No kernel may reach another device: no remote copies, remote signals or barrier semaphores. Data moves between devices by JAX's collectives and lax.ppermute only.
A program may use at most 128 MiB of HBM per device.

v0:
```python
import jax
import jax.numpy as jnp
from jax import lax
from jax.sharding import PartitionSpec as P

DEGREE = 4
filter_center = 0.25
filter_radius = 1.25


def with_halo(shard, sides, width):
    for axis, dim in sides:
        count, length = (lax.axis_size(axis), shard.shape[dim])
        up = [(i, (i + 1) % count) for i in range(count - 1)]
        down = [(j, i) for i, j in up]
        last = lax.slice_in_dim(shard, length - width, length, axis=dim)
        first = lax.slice_in_dim(shard, 0, width, axis=dim)
        before = lax.ppermute(last, axis, up)
        after = lax.ppermute(first, axis, down)
        shard = jnp.concatenate([before, shard, after], axis=dim)
    return shard


def product(vec_bf, blocks, local_index):
    block_rows = blocks.shape[0]
    size_b = blocks.shape[2]
    width = vec_bf.shape[1]
    reach = block_rows // 4
    padded = with_halo(vec_bf, (("rows", 0),), reach * size_b)
    stacked = padded.reshape(block_rows + 2 * reach, size_b, width)
    picked = stacked[local_index]
    result = jnp.einsum("rjab,rjbk->rak", blocks, picked, preferred_element_type=jnp.float32)
    return result.reshape(block_rows * size_b, width)


def split_apply(left_bf, factor):
    factor_high = factor.astype(jnp.bfloat16)
    factor_low = (factor - factor_high.astype(jnp.float32)).astype(jnp.bfloat16)
    first = jnp.dot(left_bf, factor_high.T, preferred_element_type=jnp.float32)
    second = jnp.dot(left_bf, factor_low.T, preferred_element_type=jnp.float32)
    return first + second


def shards(vectors, blocks, columns):
    block_rows = blocks.shape[0]
    reach = block_rows // 4
    first_row = lax.axis_index("rows") * block_rows
    local_index = columns - first_row + reach
    total_rows = vectors.shape[0] * lax.axis_size("rows")
    older = vectors.astype(jnp.float32)
    current = (product(vectors, blocks, local_index) - filter_center * older) / filter_radius
    for iteration in range(1, DEGREE):
        rounded = current.astype(jnp.bfloat16)
        newer = (
            2.0 * (product(rounded, blocks, local_index) - filter_center * current) / filter_radius
            - older
        )
        older = current
        current = newer
    final = current.astype(jnp.bfloat16)
    panel_width = final.shape[1]
    full_width = panel_width * lax.axis_size("vecs")
    identity = jnp.eye(full_width, dtype=jnp.float32)
    whole_block = lax.all_gather(final, "vecs", axis=1, tiled=True)
    panel = jnp.dot(final.T, whole_block, preferred_element_type=jnp.float32)
    summed = lax.psum(panel, "rows")
    gram_matrix = lax.all_gather(summed, "vecs", axis=0, tiled=True) / total_rows
    lower = jnp.linalg.cholesky(gram_matrix)
    inverse = lax.linalg.triangular_solve(lower, identity, left_side=True, lower=True)
    own_rows = lax.dynamic_slice_in_dim(
        inverse, lax.axis_index("vecs") * panel_width, panel_width, 0
    )
    return split_apply(whole_block, own_rows)


def solution(mesh):
    in_specs = (P("rows", "vecs"), P("rows", None, None, None), P("rows", None))
    out_specs = P("rows", "vecs")
    return jax.shard_map(shards, mesh=mesh, in_specs=in_specs, out_specs=out_specs, check_vma=False)
```

profile of v0, /device:TPU:1, one launch (start us, length us, event | category | flops | bytes accessed | tf_op | source)
XLA Modules:
  0.0 772.8 jit_solution(1005979501189157616)
XLA Ops:
  7.8 4.6 collective-permute-start
  15.3 3.3 collective-permute-done
  19.3 3.7 collective-permute-done.1
  25.1 7.6 gather_fusion
  32.7 7.5 fusion.88
  46.7 3.7 collective-permute-done.2
  50.4 4.4 collective-permute-done.3
  56.7 9.5 %gather_fusion.1 = bf16[160,128,256]{2,1,0:T(8,128)(2,1)} fusion(bf16[48,128,256]{2,1,0:T(8,128)(2,1)} %bitcast.194, s32[1024]{0:T(1024)S(1)} %pad_clamp_fusion), kind=kCustom, calls=%fused_computation.1 | custom fusion | bytes 20972160 | tf_op jit(solution)/shard_map/gather | solution.py:31
  66.2 7.5 fusion.89
  77.8 2.9 collective-permute-start.5
  80.7 3.2 collective-permute-done.4
  83.9 4.4 collective-permute-done.5
  90.1 9.5 %gather_fusion.2 = bf16[160,128,256]{2,1,0:T(8,128)(2,1)} fusion(bf16[48,128,256]{2,1,0:T(8,128)(2,1)} %bitcast.195, s32[1024]{0:T(1024)S(1)} %pad_clamp_fusion), kind=kCustom, calls=%fused_computation.2 | custom fusion | bytes 20972160 | tf_op jit(solution)/shard_map/gather | solution.py:31
  99.6 7.5 fusion.90
  114.6 3.7 collective-permute-done.6
  118.3 6.1 collective-permute-done.7
  126.3 9.5 %gather_fusion.3 = bf16[160,128,256]{2,1,0:T(8,128)(2,1)} fusion(bf16[48,128,256]{2,1,0:T(8,128)(2,1)} %bitcast.193, s32[1024]{0:T(1024)S(1)} %pad_clamp_fusion), kind=kCustom, calls=%fused_computation.3 | custom fusion | bytes 20972160 | tf_op jit(solution)/shard_map/gather | solution.py:31
  135.7 7.5 fusion.91
  144.9 4.4 fusion.3
  149.4 94.6 %all-gather.3.cloned.1.call-done = bf16[4096,1024]{1,0:T(8,128)(2,1)} async-done(((bf16[4096,256]{1,0:T(8,128)(2,1)}), bf16[4096,1024]{1,0:T(8,128)(2,1)}) %all-gather.3.cloned.1.call-update) | async-done | bytes 8388624 | tf_op jit(solution)/shard_map/all_gather | solution.py:64
  244.0 8.4 %fusion.87 = f32[256,1024]{0,1:T(8,128)} fusion(bf16[4096,256]{1,0:T(8,128)(2,1)} %fusion.3, bf16[4096,1024]{1,0:T(8,128)(2,1)} %all-gather.3.cloned.1.call-done), kind=kOutput, calls=%fused_computation.195 | convolution fusion | flops 2147483648 | bytes 11534336 | tf_op jit(solution)/shard_map/dot_general | solution.py:65
  252.5 106.3 %all-reduce.3.cloned.1.call-done = f32[256,1024]{0,1:T(8,128)} async-done(((f32[256,1024]{0,1:T(8,128)}), f32[256,1024]{0,1:T(8,128)}) %all-reduce.3.cloned.1.call-update) | async-done | bytes 1048592 | tf_op jit(solution)/shard_map/psum | solution.py:66
  361.7 46.9 %all-gather.5.cloned.1.call-done = f32[1024,1024]{0,1:T(8,128)} async-done(((f32[256,1024]{0,1:T(8,128)}), f32[1024,1024]{0,1:T(8,128)}) %all-gather.5.cloned.1.call-update) | async-done | bytes 4194320 | tf_op jit(solution)/shard_map/all_gather | solution.py:67
  408.6 5.0 broadcast_multiply_fusion
  413.6 5.5 copy.8
  419.1 4.4 fusion.7
  425.5 11.7 %cholesky.223 = f32[128,128]{1,0:T(8,128)S(1)} custom-call(f32[128,128]{1,0:T(8,128)S(1)} %cholesky.580), custom_call_target="Cholesky" | custom-call | tf_op jit(solution)/shard_map/jit(cholesky)/cholesky | solution.py:68
  437.3 9.8 %custom-call.62 = f32[1,128,128]{1,2,0:T(8,128)S(1)} custom-call(f32[1,128,128]{2,1,0:T(8,128)S(1)} %get-tuple-element.77), custom_call_target="InvertDiagBlocksLowerTriangular" | custom-call | tf_op jit(solution)/shard_map/jit(cholesky)/cholesky | solution.py:68
  453.5 11.9 %cholesky.244 = f32[128,128]{1,0:T(8,128)S(1)} custom-call(f32[128,128]{1,0:T(8,128)S(1)} %cholesky.584), custom_call_target="Cholesky" | custom-call | tf_op jit(solution)/shard_map/jit(cholesky)/cholesky | solution.py:68
  466.1 9.8 %custom-call.63 = f32[1,128,128]{1,2,0:T(8,128)S(1)} custom-call(f32[1,128,128]{2,1,0:T(8,128)S(1)} %get-tuple-element.74), custom_call_target="InvertDiagBlocksLowerTriangular" | custom-call | tf_op jit(solution)/shard_map/jit(cholesky)/cholesky | solution.py:68
  479.2 11.7 %cholesky.468 = f32[128,128]{1,0:T(8,128)S(1)} custom-call(f32[128,128]{1,0:T(8,128)S(1)} %cholesky.589), custom_call_target="Cholesky" | custom-call | tf_op jit(solution)/shard_map/jit(cholesky)/cholesky | solution.py:68
  492.2 9.8 %custom-call.64 = f32[1,128,128]{1,2,0:T(8,128)S(1)} custom-call(f32[1,128,128]{2,1,0:T(8,128)S(1)} %get-tuple-element.71), custom_call_target="InvertDiagBlocksLowerTriangular" | custom-call | tf_op jit(solution)/shard_map/jit(cholesky)/cholesky | solution.py:68
  505.5 12.1 %cholesky.487 = f32[128,128]{1,0:T(8,128)S(1)} custom-call(f32[128,128]{1,0:T(8,128)S(1)} %cholesky.594), custom_call_target="Cholesky" | custom-call | tf_op jit(solution)/shard_map/jit(cholesky)/cholesky | solution.py:68
  519.0 9.8 %custom-call.65 = f32[1,128,128]{1,2,0:T(8,128)S(1)} custom-call(f32[1,128,128]{2,1,0:T(8,128)S(1)} %get-tuple-element.68), custom_call_target="InvertDiagBlocksLowerTriangular" | custom-call | tf_op jit(solution)/shard_map/jit(cholesky)/cholesky | solution.py:68
  532.2 11.7 %cholesky.506 = f32[128,128]{1,0:T(8,128)S(1)} custom-call(f32[128,128]{1,0:T(8,128)S(1)} %cholesky.599), custom_call_target="Cholesky" | custom-call | tf_op jit(solution)/shard_map/jit(cholesky)/cholesky | solution.py:68
  545.2 10.0 %custom-call.66 = f32[1,128,128]{1,2,0:T(8,128)S(1)} custom-call(f32[1,128,128]{2,1,0:T(8,128)S(1)} %get-tuple-element.65), custom_call_target="InvertDiagBlocksLowerTriangular" | custom-call | tf_op jit(solution)/shard_map/jit(cholesky)/cholesky | solution.py:68
  558.5 11.7 %cholesky.526 = f32[128,128]{1,0:T(8,128)S(1)} custom-call(f32[128,128]{1,0:T(8,128)S(1)} %cholesky.604), custom_call_target="Cholesky" | custom-call | tf_op jit(solution)/shard_map/jit(cholesky)/cholesky | solution.py:68
  571.5 9.8 %custom-call.67 = f32[1,128,128]{1,2,0:T(8,128)S(1)} custom-call(f32[1,128,128]{2,1,0:T(8,128)S(1)} %get-tuple-element.62), custom_call_target="InvertDiagBlocksLowerTriangular" | custom-call | tf_op jit(solution)/shard_map/jit(cholesky)/cholesky | solution.py:68
  584.2 11.9 %cholesky.546 = f32[128,128]{1,0:T(8,128)S(1)} custom-call(f32[128,128]{1,0:T(8,128)S(1)} %cholesky.609), custom_call_target="Cholesky" | custom-call | tf_op jit(solution)/shard_map/jit(cholesky)/cholesky | solution.py:68
  597.5 9.8 %custom-call.68 = f32[1,128,128]{1,2,0:T(8,128)S(1)} custom-call(f32[1,128,128]{2,1,0:T(8,128)S(1)} %get-tuple-element.59), custom_call_target="InvertDiagBlocksLowerTriangular" | custom-call | tf_op jit(solution)/shard_map/jit(cholesky)/cholesky | solution.py:68
  609.9 11.7 %cholesky.564 = f32[128,128]{1,0:T(8,128)S(1)} custom-call(f32[128,128]{1,0:T(8,128)S(1)} %convolution_subtract_fusion.11), custom_call_target="Cholesky" | custom-call | tf_op jit(solution)/shard_map/jit(cholesky)/cholesky | solution.py:68
  628.6 4.9 select_select_fusion
  633.4 23.9 %while.1 = (s32[]{:T(128)}, f32[1024,1024]{1,0:T(8,128)}, s32[8,2]{0,1:T(2,128)S(1)}, f32[8,128,128]{2,1,0:T(8,128)S(1)}, s32[]{:T(128)}) while((s32[]{:T(128)}, f32[1024,1024]{1,0:T(8,128)}, s32[8,2]{0,1:T(2,128)S(1)}, f32[8,128,128]{2,1,0:T(8,128)S(1)}, s32[]{:T(128)}) %tuple.61), condition=%wide.while_cond, body=%wide.while_body.sunk | while | flops 2 | bytes 131189 | solution.py:69
  657.3 79.0 %custom-call.69 = f32[8,128,128]{1,2,0:T(8,128)S(1)} custom-call(f32[8,128,128]{2,1,0:T(8,128)S(1)} %get-tuple-element.12), custom_call_target="InvertDiagBlocksLowerTriangular" | custom-call | tf_op jit(solution)/shard_map/triangular_solve | solution.py:69
  747.7 2.8 convolution_subtract_fusion.2
  751.2 3.0 convolution_subtract_fusion.1
  754.9 3.4 convolution_subtract_fusion.3
  761.4 4.7 convolution_add_fusion
  (137 shorter events, 111.1 us)
Async XLA Ops:
  6.5 237.5 %all-gather.3.cloned.1.call-start = ((), (), s32[]{:S(2)}) async-start(), calls=%async_computation | async-start | bytes 10485760 | tf_op jit(solution)/shard_map/all_gather | solution.py:64
  7.8 10.7 %collective-permute-start = (bf16[1024,256]{1,0:T(8,128)(2,1)S(1)}, bf16[1024,256]{1,0:T(8,128)(2,1)S(1)}, u32[]{:S(2)}, u32[]{:S(2)}) collective-permute-start(bf16[1024,256]{1,0:T(8,128)(2,1)S(1)} %get-tuple-element.29), channel_id=1, source_target_pairs={{0,4},{4,8},{8,12},{12,16},{16,20},{20,24},{24,28},{28,32},{32,36}... | collective-permute-start | bytes 1572872 | tf_op jit(solution)/shard_map/ppermute | solution.py:18
  12.4 10.6 %collective-permute-start.1 = (bf16[1024,256]{1,0:T(8,128)(2,1)S(1)}, bf16[1024,256]{1,0:T(8,128)(2,1)}, u32[]{:S(2)}, u32[]{:S(2)}) collective-permute-start(bf16[1024,256]{1,0:T(8,128)(2,1)S(1)} %get-tuple-element.30), channel_id=1, source_target_pairs={{4,0},{8,4},{12,8},{16,12},{20,16},{24,20},{28,24},{32,28},{36,32}... | collective-permute-start | bytes 1572872 | tf_op jit(solution)/shard_map/ppermute | solution.py:19
  18.5 0.8 copy-start.12
  32.7 7.5 copy-start.7
  40.3 2.0 copy-start
  42.4 8.0 %collective-permute-start.2 = (bf16[1024,256]{1,0:T(8,128)(2,1)S(1)}, bf16[1024,256]{1,0:T(8,128)(2,1)S(1)}, u32[]{:S(2)}, u32[]{:S(2)}) collective-permute-start(bf16[1024,256]{1,0:T(8,128)(2,1)S(1)} %get-tuple-element.27), channel_id=1, source_target_pairs={{0,4},{4,8},{8,12},{12,16},{16,20},{20,24},{24,28},{28,32},{32,36}... | collective-permute-start | bytes 1572872 | tf_op jit(solution)/shard_map/ppermute | solution.py:18
  44.3 10.5 %collective-permute-start.3 = (bf16[1024,256]{1,0:T(8,128)(2,1)S(1)}, bf16[1024,256]{1,0:T(8,128)(2,1)S(1)}, u32[]{:S(2)}, u32[]{:S(2)}) collective-permute-start(bf16[1024,256]{1,0:T(8,128)(2,1)S(1)} %get-tuple-element.28), channel_id=1, source_target_pairs={{4,0},{8,4},{12,8},{16,12},{20,16},{24,20},{28,24},{32,28},{36,32}... | collective-permute-start | bytes 1572872 | tf_op jit(solution)/shard_map/ppermute | solution.py:19
  66.2 7.5 copy-start.1
  73.7 2.1 copy-start.4
  75.9 8.0 %collective-permute-start.4 = (bf16[1024,256]{1,0:T(8,128)(2,1)S(1)}, bf16[1024,256]{1,0:T(8,128)(2,1)S(1)}, u32[]{:S(2)}, u32[]{:S(2)}) collective-permute-start(bf16[1024,256]{1,0:T(8,128)(2,1)S(1)} %get-tuple-element.25), channel_id=1, source_target_pairs={{0,4},{4,8},{8,12},{12,16},{16,20},{20,24},{24,28},{28,32},{32,36}... | collective-permute-start | bytes 1572872 | tf_op jit(solution)/shard_map/ppermute | solution.py:18
  77.8 10.5 %collective-permute-start.5 = (bf16[1024,256]{1,0:T(8,128)(2,1)S(1)}, bf16[1024,256]{1,0:T(8,128)(2,1)S(1)}, u32[]{:S(2)}, u32[]{:S(2)}) collective-permute-start(bf16[1024,256]{1,0:T(8,128)(2,1)S(1)} %get-tuple-element.26), channel_id=1, source_target_pairs={{4,0},{8,4},{12,8},{16,12},{20,16},{24,20},{28,24},{32,28},{36,32}... | collective-permute-start | bytes 1572872 | tf_op jit(solution)/shard_map/ppermute | solution.py:19
  99.6 7.5 copy-start.2
  99.6 8.0 %copy-start.5 = (f32[32,256,128,1]{1,2,3,0:T(8,128)S(1)}, f32[32,256,128,1]{1,2,3,0:T(8,128)}, u32[]{:S(2)}) copy-start(f32[32,256,128,1]{1,2,3,0:T(8,128)} %copy-done.4) | copy-start | bytes 12582916
  107.6 2.6 copy-start.8
  110.3 8.0 %collective-permute-start.6 = (bf16[1024,256]{1,0:T(8,128)(2,1)S(1)}, bf16[1024,256]{1,0:T(8,128)(2,1)S(1)}, u32[]{:S(2)}, u32[]{:S(2)}) collective-permute-start(bf16[1024,256]{1,0:T(8,128)(2,1)S(1)} %get-tuple-element.23), channel_id=1, source_target_pairs={{0,4},{4,8},{8,12},{12,16},{16,20},{20,24},{24,28},{28,32},{32,36}... | collective-permute-start | bytes 1572872 | tf_op jit(solution)/shard_map/ppermute | solution.py:18
  112.2 12.2 %collective-permute-start.7 = (bf16[1024,256]{1,0:T(8,128)(2,1)S(1)}, bf16[1024,256]{1,0:T(8,128)(2,1)S(1)}, u32[]{:S(2)}, u32[]{:S(2)}) collective-permute-start(bf16[1024,256]{1,0:T(8,128)(2,1)S(1)} %get-tuple-element.24), channel_id=1, source_target_pairs={{4,0},{8,4},{12,8},{16,12},{20,16},{24,20},{28,24},{32,28},{36,32}... | collective-permute-start | bytes 1572872 | tf_op jit(solution)/shard_map/ppermute | solution.py:19
  135.7 7.5 copy-start.3
  135.7 8.0 %copy-start.6 = (f32[32,256,128,1]{1,2,3,0:T(8,128)S(1)}, f32[32,256,128,1]{1,2,3,0:T(8,128)}, u32[]{:S(2)}) copy-start(f32[32,256,128,1]{1,2,3,0:T(8,128)} %copy-done.4) | copy-start | bytes 12582916
  135.7 9.2 %copy-start.9 = (f32[32,256,128,1]{1,2,3,0:T(8,128)S(1)}, f32[32,256,128,1]{1,2,3,0:T(8,128)}, u32[]{:S(2)}) copy-start(f32[32,256,128,1]{1,2,3,0:T(8,128)} %copy-done.8) | copy-start | bytes 12582916
  149.3 209.5 %all-reduce.3.cloned.1.call-start = ((), (), s32[]{:S(2)}) async-start(), calls=%async_computation.1 | async-start | bytes 2097152 | tf_op jit(solution)/shard_map/psum | solution.py:66
  252.5 156.1 %all-gather.5.cloned.1.call-start = ((), (), s32[]{:S(2)}) async-start(), calls=%async_computation.2 | async-start | bytes 5242880 | tf_op jit(solution)/shard_map/all_gather | solution.py:67
  423.6 1.9 copy-start.11
  736.3 3.2 copy-start.10
  747.7 11.2 %slice-start = ((s8[8388608]{0:T(1024)(128)(4,1)}), s8[4194304]{0:T(1024)(128)(4,1)S(1)}, s32[]{:S(2)}) async-start(s8[8388608]{0:T(1024)(128)(4,1)} %bitcast.197), calls=%async_computation.3 | async-start | bytes 8388608
  751.2 7.7 slice-start.1
Sparse Core Ops, SparseCore 0:
  149.5 94.5 all-gather.2
  252.6 106.2 all-reduce.2
  360.6 47.9 all-gather.4
where the time goes:
time: 782 us; the launch traced here: 773 us
  other arithmetic  287 us (37%)
  waiting for transfers between devices  280 us (36%)
  matrix products  91 us (12%)
  local copies, waits for them, and re-layouts  75.8 us (10%)
  starting transfers between devices  20.1 us (3%)
  between operations  18.8 us (2%)
    another operation x30, other arithmetic, shards(): lower = jnp.linalg.cholesky(gram_matrix)  172 us
    psum x1, waiting for transfers between devices, shards(): summed = lax.psum(panel, 'rows')  106 us
    all_gather x1, waiting for transfers between devices, shards(): whole_block = lax.all_gather(final, 'vecs', axis=1, tiled=True)  94.6 us
    another operation x3, other arithmetic, shards(): lax.linalg.triangular_solve(lower, identity, left_side=True, lower=True)  83.9 us
    all_gather x1, waiting for transfers between devices, shards(): lax.all_gather(summed, 'vecs', axis=0, tiled=True) / total_rows  46.9 us
    gather x4, local copies, waits for them, and re-layouts, product(): picked = stacked[local_index]  36.1 us
    dot_general x4, matrix products, product(): jnp.einsum('rjab,rjbk->rak', blocks, picked, preferred_element_type=jnp.f...  30.1 us
    another operation x24, local copies, waits for them, and re-layouts  23.8 us
  transfers between devices with their start and end apart: 11, of which 11 were waited for; matrix products, arithmetic and copies ran while one was open for 0% of the time, Pallas kernels for 0%

commit v1 on v0

--- a/solution.py
+++ b/solution.py
@@ -63,7 +63,17 @@
     identity = jnp.eye(full_width, dtype=jnp.float32)
     whole_block = lax.all_gather(final, "vecs", axis=1, tiled=True)
     panel = jnp.dot(final.T, whole_block, preferred_element_type=jnp.float32)
-    summed = lax.psum(panel, "rows")
+
+    def close_tails(frame):
+        n_peers_all = lax.axis_size("rows")
+        even = frame
+        for i0 in [dev for dev in (1, 2, 4, 8, 16) if dev < n_peers_all]:
+            even = even + lax.ppermute(
+                even, axis_name="rows", perm=[(ix, ix ^ i0) for ix in range(n_peers_all)]
+            )
+        return even
+
+    summed = close_tails(panel)
     gram_matrix = lax.all_gather(summed, "vecs", axis=0, tiled=True) / total_rows
     lower = jnp.linalg.cholesky(gram_matrix)
     inverse = lax.linalg.triangular_solve(lower, identity, left_side=True, lower=True)

time: 782 us -> 777 us (level)
  waiting for transfers between devices: 280 us -> 265 us
  starting transfers between devices: 20.1 us -> 30.5 us
    psum x1 -> x0, waiting for transfers between devices: 106 us -> none  [shards(): summed = lax.psum(panel, 'rows')]
    ppermute x0 -> x5, waiting for transfers between devices: none -> 90.4 us  [close_tails(): lax.ppermute(even, axis_name='rows', perm=[(ix, ix ^ i0) for ix in range(...]
    ppermute x0 -> x5, starting transfers between devices: none -> 10.1 us  [close_tails(): lax.ppermute(even, axis_name='rows', perm=[(ix, ix ^ i0) for ix in range(...]
  transfers between devices with their start and end apart: 11 -> 15, of which waited for: 11 -> 15; matrix products, arithmetic and copies ran while one was open for 0% -> 0% of each run, Pallas kernels for 0% -> 0%
where the time goes in v1:
time: 777 us; the launch traced here: 768 us
  other arithmetic  288 us (37%)
  waiting for transfers between devices  265 us (34%)
  matrix products  90.2 us (12%)
  local copies, waits for them, and re-layouts  75 us (10%)
  starting transfers between devices  30.5 us (4%)
  between operations  19.3 us (2%)
    another operation x30, other arithmetic, shards(): lower = jnp.linalg.cholesky(gram_matrix)  173 us
    all_gather x1, waiting for transfers between devices, shards(): whole_block = lax.all_gather(final, 'vecs', axis=1, tiled=True)  94.1 us
    ppermute x5, waiting for transfers between devices, close_tails(): lax.ppermute(even, axis_name='rows', perm=[(ix, ix ^ i0) for ix in range(...  90.4 us
    another operation x3, other arithmetic, shards(): lax.linalg.triangular_solve(lower, identity, left_side=True, lower=True)  83.9 us
    all_gather x1, waiting for transfers between devices, shards(): lax.all_gather(summed, 'vecs', axis=0, tiled=True) / total_rows  48 us
    gather x4, local copies, waits for them, and re-layouts, product(): picked = stacked[local_index]  36.1 us
    dot_general x4, matrix products, product(): jnp.einsum('rjab,rjbk->rak', blocks, picked, preferred_element_type=jnp.f...  30.1 us
    another operation x14, matrix products, shards(): lower = jnp.linalg.cholesky(gram_matrix)  23.1 us
  transfers between devices with their start and end apart: 15, of which 15 were waited for; matrix products, arithmetic and copies ran while one was open for 0% of the time, Pallas kernels for 0%

profile of v1, /device:TPU:1, one launch (start us, length us, event | category | flops | bytes accessed | tf_op | source)
XLA Modules:
  0.0 768.5 jit_solution(15062721935047281479)
XLA Ops:
  7.8 4.6 collective-permute-start
  15.3 3.3 collective-permute-done
  19.3 3.7 collective-permute-done.1
  25.1 7.6 gather_fusion
  32.7 7.5 fusion.105
  46.8 3.7 collective-permute-done.2
  50.4 4.4 collective-permute-done.3
  56.7 9.5 %gather_fusion.1 = bf16[160,128,256]{2,1,0:T(8,128)(2,1)} fusion(bf16[48,128,256]{2,1,0:T(8,128)(2,1)} %bitcast.194, s32[1024]{0:T(1024)S(1)} %pad_clamp_fusion), kind=kCustom, calls=%fused_computation.1 | custom fusion | bytes 20972160 | tf_op jit(solution)/shard_map/gather | solution.py:31
  66.2 7.5 fusion.106
  80.5 3.4 collective-permute-done.4
  83.9 4.4 collective-permute-done.5
  90.1 9.5 %gather_fusion.2 = bf16[160,128,256]{2,1,0:T(8,128)(2,1)} fusion(bf16[48,128,256]{2,1,0:T(8,128)(2,1)} %bitcast.195, s32[1024]{0:T(1024)S(1)} %pad_clamp_fusion), kind=kCustom, calls=%fused_computation.2 | custom fusion | bytes 20972160 | tf_op jit(solution)/shard_map/gather | solution.py:31
  99.6 7.5 fusion.107
  114.7 3.7 collective-permute-done.6
  118.3 6.1 collective-permute-done.7
  126.3 9.5 %gather_fusion.3 = bf16[160,128,256]{2,1,0:T(8,128)(2,1)} fusion(bf16[48,128,256]{2,1,0:T(8,128)(2,1)} %bitcast.193, s32[1024]{0:T(1024)S(1)} %pad_clamp_fusion), kind=kCustom, calls=%fused_computation.3 | custom fusion | bytes 20972160 | tf_op jit(solution)/shard_map/gather | solution.py:31
  135.8 7.5 fusion.108
  145.0 4.4 fusion.3
  150.0 94.1 %all-gather.3.cloned.1.call-done = bf16[4096,1024]{1,0:T(8,128)(2,1)} async-done(((bf16[4096,256]{1,0:T(8,128)(2,1)}), bf16[4096,1024]{1,0:T(8,128)(2,1)}) %all-gather.3.cloned.1.call-update) | async-done | bytes 8388624 | tf_op jit(solution)/shard_map/all_gather | solution.py:64
  244.1 7.4 fusion.104
  256.8 23.2 %collective-permute-done.9 = f32[256,1024]{0,1:T(8,128)S(1)} collective-permute-done((f32[256,1024]{0,1:T(8,128)S(1)}, f32[256,1024]{0,1:T(8,128)S(1)}, u32[]{:S(2)}, u32[]{:S(2)}) %collective-permute-start.9) | collective-permute-done | bytes 1048608 | tf_op jit(solution)/shard_map/ppermute | solution.py:71
  283.0 22.2 %collective-permute-done.10 = f32[256,1024]{0,1:T(8,128)S(1)} collective-permute-done((f32[256,1024]{0,1:T(8,128)S(1)}, f32[256,1024]{0,1:T(8,128)S(1)}, u32[]{:S(2)}, u32[]{:S(2)}) %collective-permute-start.10) | collective-permute-done | bytes 1048608 | tf_op jit(solution)/shard_map/ppermute | solution.py:71
  306.7 21.3 %collective-permute-done.11 = f32[256,1024]{0,1:T(8,128)S(1)} collective-permute-done((f32[256,1024]{0,1:T(8,128)S(1)}, f32[256,1024]{0,1:T(8,128)S(1)}, u32[]{:S(2)}, u32[]{:S(2)}) %collective-permute-start.11) | collective-permute-done | bytes 1048608 | tf_op jit(solution)/shard_map/ppermute | solution.py:71
  331.0 21.4 %collective-permute-done.12 = f32[256,1024]{0,1:T(8,128)S(1)} collective-permute-done((f32[256,1024]{0,1:T(8,128)S(1)}, f32[256,1024]{0,1:T(8,128)S(1)}, u32[]{:S(2)}, u32[]{:S(2)}) %collective-permute-start.12) | collective-permute-done | bytes 1048608 | tf_op jit(solution)/shard_map/ppermute | solution.py:71
  356.4 48.0 %all-gather.5.cloned.1.call-done = f32[1024,1024]{0,1:T(8,128)} async-done(((f32[256,1024]{0,1:T(8,128)}), f32[1024,1024]{0,1:T(8,128)}) %all-gather.5.cloned.1.call-update) | async-done | bytes 4194320 | tf_op jit(solution)/shard_map/all_gather | solution.py:77
  404.4 5.0 broadcast_multiply_fusion
  409.4 5.5 copy.10
  415.0 4.4 fusion.7
  421.5 11.7 %cholesky.223 = f32[128,128]{1,0:T(8,128)S(1)} custom-call(f32[128,128]{1,0:T(8,128)S(1)} %cholesky.580), custom_call_target="Cholesky" | custom-call | tf_op jit(solution)/shard_map/jit(cholesky)/cholesky | solution.py:78
  433.2 9.8 %custom-call.62 = f32[1,128,128]{1,2,0:T(8,128)S(1)} custom-call(f32[1,128,128]{2,1,0:T(8,128)S(1)} %get-tuple-element.77), custom_call_target="InvertDiagBlocksLowerTriangular" | custom-call | tf_op jit(solution)/shard_map/jit(cholesky)/cholesky | solution.py:78
  449.4 11.9 %cholesky.244 = f32[128,128]{1,0:T(8,128)S(1)} custom-call(f32[128,128]{1,0:T(8,128)S(1)} %cholesky.584), custom_call_target="Cholesky" | custom-call | tf_op jit(solution)/shard_map/jit(cholesky)/cholesky | solution.py:78
  462.0 9.8 %custom-call.63 = f32[1,128,128]{1,2,0:T(8,128)S(1)} custom-call(f32[1,128,128]{2,1,0:T(8,128)S(1)} %get-tuple-element.74), custom_call_target="InvertDiagBlocksLowerTriangular" | custom-call | tf_op jit(solution)/shard_map/jit(cholesky)/cholesky | solution.py:78
  475.2 11.7 %cholesky.468 = f32[128,128]{1,0:T(8,128)S(1)} custom-call(f32[128,128]{1,0:T(8,128)S(1)} %cholesky.589), custom_call_target="Cholesky" | custom-call | tf_op jit(solution)/shard_map/jit(cholesky)/cholesky | solution.py:78
  488.2 9.8 %custom-call.64 = f32[1,128,128]{1,2,0:T(8,128)S(1)} custom-call(f32[1,128,128]{2,1,0:T(8,128)S(1)} %get-tuple-element.71), custom_call_target="InvertDiagBlocksLowerTriangular" | custom-call | tf_op jit(solution)/shard_map/jit(cholesky)/cholesky | solution.py:78
  501.5 12.1 %cholesky.487 = f32[128,128]{1,0:T(8,128)S(1)} custom-call(f32[128,128]{1,0:T(8,128)S(1)} %cholesky.594), custom_call_target="Cholesky" | custom-call | tf_op jit(solution)/shard_map/jit(cholesky)/cholesky | solution.py:78
  515.0 9.8 %custom-call.65 = f32[1,128,128]{1,2,0:T(8,128)S(1)} custom-call(f32[1,128,128]{2,1,0:T(8,128)S(1)} %get-tuple-element.68), custom_call_target="InvertDiagBlocksLowerTriangular" | custom-call | tf_op jit(solution)/shard_map/jit(cholesky)/cholesky | solution.py:78
  528.3 11.7 %cholesky.506 = f32[128,128]{1,0:T(8,128)S(1)} custom-call(f32[128,128]{1,0:T(8,128)S(1)} %cholesky.599), custom_call_target="Cholesky" | custom-call | tf_op jit(solution)/shard_map/jit(cholesky)/cholesky | solution.py:78
  541.3 10.0 %custom-call.66 = f32[1,128,128]{1,2,0:T(8,128)S(1)} custom-call(f32[1,128,128]{2,1,0:T(8,128)S(1)} %get-tuple-element.65), custom_call_target="InvertDiagBlocksLowerTriangular" | custom-call | tf_op jit(solution)/shard_map/jit(cholesky)/cholesky | solution.py:78
  554.6 11.7 %cholesky.526 = f32[128,128]{1,0:T(8,128)S(1)} custom-call(f32[128,128]{1,0:T(8,128)S(1)} %cholesky.604), custom_call_target="Cholesky" | custom-call | tf_op jit(solution)/shard_map/jit(cholesky)/cholesky | solution.py:78
  567.6 9.8 %custom-call.67 = f32[1,128,128]{1,2,0:T(8,128)S(1)} custom-call(f32[1,128,128]{2,1,0:T(8,128)S(1)} %get-tuple-element.62), custom_call_target="InvertDiagBlocksLowerTriangular" | custom-call | tf_op jit(solution)/shard_map/jit(cholesky)/cholesky | solution.py:78
  580.4 11.9 %cholesky.546 = f32[128,128]{1,0:T(8,128)S(1)} custom-call(f32[128,128]{1,0:T(8,128)S(1)} %cholesky.609), custom_call_target="Cholesky" | custom-call | tf_op jit(solution)/shard_map/jit(cholesky)/cholesky | solution.py:78
  593.6 9.8 %custom-call.68 = f32[1,128,128]{1,2,0:T(8,128)S(1)} custom-call(f32[1,128,128]{2,1,0:T(8,128)S(1)} %get-tuple-element.59), custom_call_target="InvertDiagBlocksLowerTriangular" | custom-call | tf_op jit(solution)/shard_map/jit(cholesky)/cholesky | solution.py:78
  606.0 11.7 %cholesky.564 = f32[128,128]{1,0:T(8,128)S(1)} custom-call(f32[128,128]{1,0:T(8,128)S(1)} %slice_subtract_fusion.6), custom_call_target="Cholesky" | custom-call | tf_op jit(solution)/shard_map/jit(cholesky)/cholesky | solution.py:78
  624.9 4.9 select_select_fusion
  629.7 23.0 %while.1 = (s32[]{:T(128)}, f32[1024,1024]{1,0:T(8,128)}, s32[8,2]{0,1:T(2,128)S(1)}, f32[8,128,128]{2,1,0:T(8,128)S(1)}, s32[]{:T(128)}) while((s32[]{:T(128)}, f32[1024,1024]{1,0:T(8,128)}, s32[8,2]{0,1:T(2,128)S(1)}, f32[8,128,128]{2,1,0:T(8,128)S(1)}, s32[]{:T(128)}) %tuple.61), condition=%wide.while_cond, body=%wide.while_body.sunk | while | flops 2 | bytes 131189 | solution.py:79
  652.7 79.0 %custom-call.69 = f32[8,128,128]{1,2,0:T(8,128)S(1)} custom-call(f32[8,128,128]{2,1,0:T(8,128)S(1)} %get-tuple-element.12), custom_call_target="InvertDiagBlocksLowerTriangular" | custom-call | tf_op jit(solution)/shard_map/triangular_solve | solution.py:79
  750.2 3.4 convolution_subtract_fusion.3
  756.7 4.7 convolution_add_fusion
  (149 shorter events, 133.5 us)
Async XLA Ops:
  6.5 237.5 %all-gather.3.cloned.1.call-start = ((), (), s32[]{:S(2)}) async-start(), calls=%async_computation | async-start | bytes 10485760 | tf_op jit(solution)/shard_map/all_gather | solution.py:64
  7.8 10.7 %collective-permute-start = (bf16[1024,256]{1,0:T(8,128)(2,1)S(1)}, bf16[1024,256]{1,0:T(8,128)(2,1)S(1)}, u32[]{:S(2)}, u32[]{:S(2)}) collective-permute-start(bf16[1024,256]{1,0:T(8,128)(2,1)S(1)} %get-tuple-element.29), channel_id=1, source_target_pairs={{0,4},{4,8},{8,12},{12,16},{16,20},{20,24},{24,28},{28,32},{32,36}... | collective-permute-start | bytes 1572872 | tf_op jit(solution)/shard_map/ppermute | solution.py:18
  12.4 10.6 %collective-permute-start.1 = (bf16[1024,256]{1,0:T(8,128)(2,1)S(1)}, bf16[1024,256]{1,0:T(8,128)(2,1)}, u32[]{:S(2)}, u32[]{:S(2)}) collective-permute-start(bf16[1024,256]{1,0:T(8,128)(2,1)S(1)} %get-tuple-element.30), channel_id=1, source_target_pairs={{4,0},{8,4},{12,8},{16,12},{20,16},{24,20},{28,24},{32,28},{36,32}... | collective-permute-start | bytes 1572872 | tf_op jit(solution)/shard_map/ppermute | solution.py:19
  18.5 0.8 copy-start.12
  32.7 7.5 copy-start.7
  40.3 2.0 copy-start
  42.4 8.0 %collective-permute-start.2 = (bf16[1024,256]{1,0:T(8,128)(2,1)S(1)}, bf16[1024,256]{1,0:T(8,128)(2,1)S(1)}, u32[]{:S(2)}, u32[]{:S(2)}) collective-permute-start(bf16[1024,256]{1,0:T(8,128)(2,1)S(1)} %get-tuple-element.27), channel_id=1, source_target_pairs={{0,4},{4,8},{8,12},{12,16},{16,20},{20,24},{24,28},{28,32},{32,36}... | collective-permute-start | bytes 1572872 | tf_op jit(solution)/shard_map/ppermute | solution.py:18
  44.3 10.5 %collective-permute-start.3 = (bf16[1024,256]{1,0:T(8,128)(2,1)S(1)}, bf16[1024,256]{1,0:T(8,128)(2,1)S(1)}, u32[]{:S(2)}, u32[]{:S(2)}) collective-permute-start(bf16[1024,256]{1,0:T(8,128)(2,1)S(1)} %get-tuple-element.28), channel_id=1, source_target_pairs={{4,0},{8,4},{12,8},{16,12},{20,16},{24,20},{28,24},{32,28},{36,32}... | collective-permute-start | bytes 1572872 | tf_op jit(solution)/shard_map/ppermute | solution.py:19
  66.2 7.5 copy-start.1
  73.8 2.1 copy-start.4
  75.9 8.0 %collective-permute-start.4 = (bf16[1024,256]{1,0:T(8,128)(2,1)S(1)}, bf16[1024,256]{1,0:T(8,128)(2,1)S(1)}, u32[]{:S(2)}, u32[]{:S(2)}) collective-permute-start(bf16[1024,256]{1,0:T(8,128)(2,1)S(1)} %get-tuple-element.25), channel_id=1, source_target_pairs={{0,4},{4,8},{8,12},{12,16},{16,20},{20,24},{24,28},{28,32},{32,36}... | collective-permute-start | bytes 1572872 | tf_op jit(solution)/shard_map/ppermute | solution.py:18
  77.8 10.5 %collective-permute-start.5 = (bf16[1024,256]{1,0:T(8,128)(2,1)S(1)}, bf16[1024,256]{1,0:T(8,128)(2,1)S(1)}, u32[]{:S(2)}, u32[]{:S(2)}) collective-permute-start(bf16[1024,256]{1,0:T(8,128)(2,1)S(1)} %get-tuple-element.26), channel_id=1, source_target_pairs={{4,0},{8,4},{12,8},{16,12},{20,16},{24,20},{28,24},{32,28},{36,32}... | collective-permute-start | bytes 1572872 | tf_op jit(solution)/shard_map/ppermute | solution.py:19
  99.6 7.5 copy-start.2
  99.6 8.0 %copy-start.5 = (f32[32,256,128,1]{1,2,3,0:T(8,128)S(1)}, f32[32,256,128,1]{1,2,3,0:T(8,128)}, u32[]{:S(2)}) copy-start(f32[32,256,128,1]{1,2,3,0:T(8,128)} %copy-done.4) | copy-start | bytes 12582916
  107.6 2.6 copy-start.8
  110.3 8.0 %collective-permute-start.6 = (bf16[1024,256]{1,0:T(8,128)(2,1)S(1)}, bf16[1024,256]{1,0:T(8,128)(2,1)S(1)}, u32[]{:S(2)}, u32[]{:S(2)}) collective-permute-start(bf16[1024,256]{1,0:T(8,128)(2,1)S(1)} %get-tuple-element.23), channel_id=1, source_target_pairs={{0,4},{4,8},{8,12},{12,16},{16,20},{20,24},{24,28},{28,32},{32,36}... | collective-permute-start | bytes 1572872 | tf_op jit(solution)/shard_map/ppermute | solution.py:18
  112.2 12.2 %collective-permute-start.7 = (bf16[1024,256]{1,0:T(8,128)(2,1)S(1)}, bf16[1024,256]{1,0:T(8,128)(2,1)S(1)}, u32[]{:S(2)}, u32[]{:S(2)}) collective-permute-start(bf16[1024,256]{1,0:T(8,128)(2,1)S(1)} %get-tuple-element.24), channel_id=1, source_target_pairs={{4,0},{8,4},{12,8},{16,12},{20,16},{24,20},{28,24},{32,28},{36,32}... | collective-permute-start | bytes 1572872 | tf_op jit(solution)/shard_map/ppermute | solution.py:19
  135.8 7.5 copy-start.3
  135.8 8.0 %copy-start.6 = (f32[32,256,128,1]{1,2,3,0:T(8,128)S(1)}, f32[32,256,128,1]{1,2,3,0:T(8,128)}, u32[]{:S(2)}) copy-start(f32[32,256,128,1]{1,2,3,0:T(8,128)} %copy-done.4) | copy-start | bytes 12582916
  135.8 9.2 %copy-start.9 = (f32[32,256,128,1]{1,2,3,0:T(8,128)S(1)}, f32[32,256,128,1]{1,2,3,0:T(8,128)}, u32[]{:S(2)}) copy-start(f32[32,256,128,1]{1,2,3,0:T(8,128)} %copy-done.8) | copy-start | bytes 12582916
  149.4 255.0 %all-gather.5.cloned.1.call-start = ((), (), s32[]{:S(2)}) async-start(), calls=%async_computation.1 | async-start | bytes 5242880 | tf_op jit(solution)/shard_map/all_gather | solution.py:77
  251.5 4.0 collective-permute-start.8
  255.5 24.5 %collective-permute-start.9 = (f32[256,1024]{0,1:T(8,128)S(1)}, f32[256,1024]{0,1:T(8,128)S(1)}, u32[]{:S(2)}, u32[]{:S(2)}) collective-permute-start(f32[256,1024]{0,1:T(8,128)S(1)} %add.117), channel_id=1, source_target_pairs={{0,8},{4,12},{8,0},{12,4},{16,24},{20,28},{24,16},{28,20},{32,40},... | collective-permute-start | bytes 3145736 | tf_op jit(solution)/shard_map/ppermute | solution.py:71
  280.1 25.0 %collective-permute-start.10 = (f32[256,1024]{0,1:T(8,128)S(1)}, f32[256,1024]{0,1:T(8,128)S(1)}, u32[]{:S(2)}, u32[]{:S(2)}) collective-permute-start(f32[256,1024]{0,1:T(8,128)S(1)} %add.118), channel_id=1, source_target_pairs={{0,16},{4,20},{8,24},{12,28},{16,0},{20,4},{24,8},{28,12},{32,48},... | collective-permute-start | bytes 3145736 | tf_op jit(solution)/shard_map/ppermute | solution.py:71
  305.3 22.6 %collective-permute-start.11 = (f32[256,1024]{0,1:T(8,128)S(1)}, f32[256,1024]{0,1:T(8,128)S(1)}, u32[]{:S(2)}, u32[]{:S(2)}) collective-permute-start(f32[256,1024]{0,1:T(8,128)S(1)} %add.119), channel_id=1, source_target_pairs={{0,32},{4,36},{8,40},{12,44},{16,48},{20,52},{24,56},{28,60},{32,0... | collective-permute-start | bytes 3145736 | tf_op jit(solution)/shard_map/ppermute | solution.py:71
  328.1 24.4 %collective-permute-start.12 = (f32[256,1024]{0,1:T(8,128)S(1)}, f32[256,1024]{0,1:T(8,128)S(1)}, u32[]{:S(2)}, u32[]{:S(2)}) collective-permute-start(f32[256,1024]{0,1:T(8,128)S(1)} %add.120), channel_id=1, source_target_pairs={{0,64},{4,68},{8,72},{12,76},{16,80},{20,84},{24,88},{28,92},{32,9... | collective-permute-start | bytes 3145736 | tf_op jit(solution)/shard_map/ppermute | solution.py:71
  419.4 2.0 copy-start.11
  731.8 3.2 copy-start.10
  743.1 11.2 %slice-start = ((s8[8388608]{0:T(1024)(128)(4,1)}), s8[4194304]{0:T(1024)(128)(4,1)S(1)}, s32[]{:S(2)}) async-start(s8[8388608]{0:T(1024)(128)(4,1)} %bitcast.197), calls=%async_computation.2 | async-start | bytes 8388608
  746.6 7.7 %slice-start.1 = ((s8[8388608]{0:T(1024)(128)(4,1)}), s8[4194304]{0:T(1024)(128)(4,1)S(1)}, s32[]{:S(2)}) async-start(s8[8388608]{0:T(1024)(128)(4,1)} %bitcast.197), calls=%async_computation.3 | async-start | bytes 8388608
Sparse Core Ops, SparseCore 0:
  149.5 94.5 all-gather.2
  353.7 50.6 all-gather.4
